TPU v7x, 512 devices: a whole 4x8x8 slice. The times are simulated.
512 devices in a mesh: ex: 32 (over y, x_hi, core), layer: 16 (over x_lo, z).
Axes of the slice: x: 4 (x_hi: 2, x_lo: 2; x = x_hi * 2 + x_lo), y: 8, z: 8, core: 2. Of those that a mesh axis runs over, the one named last changes fastest.
Arguments:
- queries: bfloat16 [16, 1024, 4096], P('layer', 'ex'), may hold values from -6 to 6
- train_grads: bfloat16 [16, 16384, 4096], P('layer', 'ex'), may hold values from -0.09375 to 0.09375
- basis_in: float32 [16, 64, 64], P('layer'), may hold values from -0.75 to 0.75
- basis_out: float32 [16, 64, 64], P('layer'), may hold values from -0.75 to 0.75
- inverse_eigen: float32 [16, 64, 64], P('layer'), may hold values from 0.05 to 1
Outputs:
- scores: float32 [1024, 16384], P('layer', 'ex')
All inputs are finite; a program needn't handle non-finite values.
Results may differ from a plain program's by a relative error of at most 0.0029.
Values may be sent and summed in bfloat16 or wider, within the bound.
A program may use at most 64 MiB of HBM per device.

v0:
```python
import jax
import jax.numpy as jnp
from jax import lax
from jax.sharding import PartitionSpec as P


def precondition(block, basis_in, basis_out, inverse_eigen):
    count = block.shape[0]
    width_in = basis_in.shape[0]
    width_out = basis_out.shape[0]
    grads = block.astype(jnp.float32).reshape(count, width_out, width_in)
    high = lax.Precision.HIGHEST
    right = jnp.einsum("qoi,ia->qoa", grads, basis_in, precision=high)
    rotated = jnp.einsum("ob,qoa->qba", basis_out, right, precision=high)
    scaled = rotated * inverse_eigen[None]
    back = jnp.einsum("qba,ja->qbj", scaled, basis_in, precision=high)
    full = jnp.einsum("ob,qbj->qoj", basis_out, back, precision=high)
    return full.reshape(count, width_out * width_in).astype(jnp.bfloat16)


def layer_scores(query_part, train_grads):
    return lax.dot_general(
        query_part, train_grads, (((0, 2), (0, 2)), ((), ())), preferred_element_type=jnp.float32
    )


def per_device(queries, train_grads, basis_in, basis_out, inverse_eigen):
    pieces = [precondition(queries[0], basis_in[0], basis_out[0], inverse_eigen[0])]
    conditioned = jnp.stack(pieces, axis=0)
    block_scores = layer_scores(lax.all_gather(conditioned, "ex", axis=1, tiled=True), train_grads)
    return lax.psum_scatter(block_scores, "layer", scatter_dimension=0, tiled=True)


def solution(mesh):
    in_specs = (
        P("layer", "ex", None),
        P("layer", "ex", None),
        P("layer", None, None),
        P("layer", None, None),
        P("layer", None, None),
    )
    out_specs = P("layer", "ex")
    return jax.shard_map(
        per_device, mesh=mesh, in_specs=in_specs, out_specs=out_specs, check_vma=False
    )
```

profile of v0, /device:TPU:8, one launch (start us, length us, event | category | flops | bytes accessed | tf_op | source)
XLA Modules:
  0.0 219.3 jit_solution(13912658594986489597)
XLA Ops:
  6.5 0.0 copy-start
  6.5 0.0 copy-start.1
  6.5 0.0 all-gather.2.cloned.1.call-start
  6.5 0.8 copy.7
  7.4 1.5 reshape.22
  8.9 0.0 copy-done
  8.9 0.6 fusion.9
  9.4 2.6 %fusion.3 = f32[32,64,64]{1,2,0:T(8,128)S(1)} fusion(f32[32,64,64]{2,1,0:T(8,128)S(1)} %fusion.9, f32[64,64]{0,1:T(8,128)S(1)} %copy.7, f32[1,64,64]{2,1,0:T(8,128)} %param.8), kind=kOutput, calls=%fused_computation.4 | convolution fusion | flops 100794368 | bytes 1081344 | tf_op jit(solution)/shard_map/ob,qoa->qba/dot_general | solution.py:14
  12.0 1.1 fusion.7
  13.1 0.0 copy-done.1
  13.1 1.0 fusion.4
  14.1 0.3 copy.8
  14.4 1.2 convert_element_type.19
  15.6 0.0 all-gather.2.cloned.1.call-update
  15.6 0.0 reduce-scatter.2.cloned.1.call-start
  15.6 111.2 %all-gather.2.cloned.1.call-done = bf16[1,1024,4096]{2,1,0:T(8,128)(2,1)} async-done(((bf16[1,32,4096]{2,1,0:T(8,128)(2,1)}), bf16[1,1024,4096]{2,1,0:T(8,128)(2,1)}) %all-gather.2.cloned.1.call-update) | async-done | bytes 8388624 | tf_op jit(solution)/shard_map/all_gather | solution.py:30
  126.9 10.5 %fusion = f32[1024,512]{1,0:T(8,128)} fusion(bf16[1,1024,4096]{2,1,0:T(8,128)(2,1)} %all-gather.2.cloned.1.call-done, bf16[1,512,4096]{2,1,0:T(8,128)(2,1)} %param.6), kind=kOutput, calls=%fused_computation | convolution fusion | flops 4294967296 | bytes 14680064 | tf_op jit(solution)/shard_map/dot_general | solution.py:22
  137.3 0.0 reduce-scatter.2.cloned.1.call-update
  137.3 75.1 %reduce-scatter.2.cloned.1.call-done = f32[64,512]{1,0:T(8,128)} async-done(((f32[1024,512]{1,0:T(8,128)}), f32[64,512]{1,0:T(8,128)}) %reduce-scatter.2.cloned.1.call-update) | async-done | bytes 131088 | tf_op jit(solution)/shard_map/reduce_scatter | solution.py:31
Async XLA Ops:
  6.5 2.3 %copy-start = (f32[1,64,64]{2,1,0:T(8,128)S(1)}, f32[1,64,64]{2,1,0:T(8,128)}, u32[]{:S(2)}) copy-start(f32[1,64,64]{2,1,0:T(8,128)} %param.7) | copy-start | bytes 49156
  6.5 6.6 %copy-start.1 = (f32[1,64,64]{2,1,0:T(8,128)S(1)}, f32[1,64,64]{2,1,0:T(8,128)}, u32[]{:S(2)}) copy-start(f32[1,64,64]{2,1,0:T(8,128)} %param.8) | copy-start | bytes 49156
  6.5 120.3 %all-gather.2.cloned.1.call-start = ((), (), s32[]{:S(2)}) async-start(), calls=%async_computation.1 | async-start | bytes 8650752 | tf_op jit(solution)/shard_map/all_gather | solution.py:30
  15.6 196.8 %reduce-scatter.2.cloned.1.call-start = ((), (), s32[]{:S(2)}) async-start(), calls=%async_computation.2 | async-start | bytes 2228224 | tf_op jit(solution)/shard_map/reduce_scatter | solution.py:31
Sparse Core Ops, SparseCore 0:
  15.7 111.0 all-gather.1
  137.5 74.9 reduce-scatter.1
where the time goes:
time: 220 us; the launch traced here: 219 us
  waiting for transfers between devices  186 us (85%)
  matrix products  15.6 us (7%)
  between operations  13.5 us (6%)
  local copies, waits for them, and re-layouts  3.8 us (2%)
    all_gather x1, waiting for transfers between devices, per_device(): lax.all_gather(conditioned, 'ex', axis=1, tiled=True)  111 us
    reduce_scatter x1, waiting for transfers between devices, per_device(): lax.psum_scatter(block_scores, 'layer', scatter_dimension=0, tiled=True)  75.1 us
    dot_general x1, matrix products, layer_scores(): lax.dot_general(query_part, train_grads, (((0, 2), (0, 2)), ((), ())), pr...  10.5 us
  transfers between devices with their start and end apart: 2, of which 2 were waited for; matrix products, arithmetic and copies ran while one was open for 0% of the time, Pallas kernels for 0%

commit v1 on v0

v1 whole, which is shorter than its diff:
```python
import functools

import jax
import jax.numpy as jnp
from jax import lax
from jax.experimental import pallas as pl
from jax.experimental.pallas import tpu as pltpu
from jax.sharding import PartitionSpec as P

MESH = pl.DeviceIdType.MESH
NY, NH, NC = 8, 2, 2
NL, NZ = 2, 8
HALF = 16
WIDTH = 64
GRAD = WIDTH * WIDTH
LANES = 128
PAIRS = GRAD // LANES
BLOCK = 64
COLS = 512
F32, BF16 = jnp.float32, jnp.bfloat16


def split(value):
    high = value.astype(BF16)
    return high, (value - high.astype(F32)).astype(BF16)


def dot(left, right, dims=((1,), (0,))):
    return lax.dot_general(left, right, (dims, ((), ())), preferred_element_type=F32)


def twice(value):
    return jnp.concatenate([value, value], axis=1)


def lower_half(shape):
    return lax.rem(lax.broadcasted_iota(jnp.int32, shape, 1), LANES) < WIDTH


def weights(bi_ref, bo_ref, eig_ref):
    wide = twice(bi_ref[...])
    low = lower_half(wide.shape)
    diag = jnp.concatenate([jnp.where(low, wide, 0.0), jnp.where(low, 0.0, wide)], axis=0)
    diag_hi, diag_lo = split(diag)
    first = jnp.concatenate([diag_hi, diag_lo], axis=0)
    last = jnp.concatenate([diag_hi, diag_hi, diag_lo], axis=1)
    even, odd = bo_ref[pl.ds(0, PAIRS, stride=2), :], bo_ref[pl.ds(1, PAIRS, stride=2), :]
    rows = jnp.concatenate([even, odd], axis=1)
    rows_hi = rows.astype(BF16).astype(F32)
    rows_lo = rows - rows_hi
    into = jnp.transpose(jnp.concatenate([rows_hi, rows_hi, rows_lo, rows_lo], axis=0)).astype(BF16)
    stack = jnp.concatenate([even, odd], axis=0)
    stack_hi = stack.astype(BF16).astype(F32)
    back = jnp.concatenate([twice(stack_hi), twice(stack - stack_hi)], axis=1).astype(BF16)
    return first, into, twice(eig_ref[...]), back, last


def precondition(block, mats, rows_ref, turned_ref):
    first, into, eig, back, last = mats
    stacked = jnp.concatenate([block[:, p * LANES : (p + 1) * LANES] for p in range(PAIRS)], axis=0)
    rows_ref[...] = dot(jnp.concatenate([stacked, stacked], axis=1), first)
    right = jnp.concatenate([rows_ref[pl.ds(q, PAIRS, stride=HALF), :] for q in range(HALF)], axis=1)
    right_hi, right_lo = split(right)
    both = dot(into, jnp.concatenate([right_hi, right_lo, right_hi, right_lo], axis=0))
    low = lower_half((WIDTH, HALF * LANES))
    picked = jnp.where(low, both[:WIDTH], both[WIDTH:])
    scaled = []
    for q in range(HALF):
        part = picked[:, q * LANES : (q + 1) * LANES]
        scaled.append((part + pltpu.roll(part, WIDTH, 1)) * eig)
    scaled_hi, scaled_lo = split(jnp.concatenate(scaled, axis=1))
    left = dot(back, jnp.concatenate([scaled_hi, scaled_lo, scaled_hi, scaled_lo], axis=0))
    left = jnp.where(lower_half((PAIRS, HALF * LANES)), left[:PAIRS], left[PAIRS:])
    left = jnp.concatenate([left[:, q * LANES : (q + 1) * LANES] for q in range(HALF)], axis=0)
    left_hi, left_lo = split(left)
    full = dot(jnp.concatenate([left_hi, left_lo, left_hi], axis=1), last, ((1,), (1,)))
    for q in range(HALF):
        turned_ref[pl.ds(q, PAIRS, stride=HALF), :] = full[q * PAIRS : (q + 1) * PAIRS]
    return [turned_ref[p * HALF : (p + 1) * HALF, :].astype(BF16) for p in range(PAIRS)]


def kernel(
    q_hbm, t_hbm, bi_ref, bo_ref, eig_ref, out_ref,
    q_ref, t_ref, cond, outbox, inbox, xbox, sums, rows_ref, turned_ref,
    load_sem, y_send, y_recv, y4_send, y4_recv, x_send, x_recv, s_send, s_recv, z_send, z_recv, l_send, l_recv,
):
    ex, layer = lax.axis_index("ex"), lax.axis_index("layer")
    y, h, c = ex // (NH * NC), lax.rem(ex // NC, NH), lax.rem(ex, NC)
    lo, z = layer // NZ, lax.rem(layer, NZ)

    def device(yy, hh, cc, ll, zz):
        return ((yy * NH + hh) * NC + cc, ll * NZ + zz)

    y_next = device(lax.rem(y + 1, NY), h, c, lo, z)
    y_prev = device(lax.rem(y + NY - 1, NY), h, c, lo, z)
    x_peer = device(y, 1 - h, c, lo, z)
    sibling = device(y, h, 1 - c, lo, z)
    lo_peer = device(y, h, c, 1 - lo, z)

    loads = [
        pltpu.make_async_copy(q_hbm.at[0], q_ref, load_sem.at[0]),
        pltpu.make_async_copy(t_hbm.at[0], t_ref, load_sem.at[1]),
    ]
    for load in loads:
        load.start()

    barrier = pltpu.get_barrier_semaphore()
    for peer in (y_next, y_prev, x_peer, sibling, lo_peer):
        pl.semaphore_signal(barrier, inc=1, device_id=peer, device_id_type=MESH)

    def greet(k, _):
        pl.semaphore_signal(
            barrier, inc=1, device_id=device(y, h, c, lo, lax.rem(z + k, NZ)), device_id_type=MESH
        )
        return 0

    lax.fori_loop(1, NZ, greet, 0)

    def rows_at(place, hh, cc, half):
        start = ((place * NH + hh) * NC + cc) * (2 * HALF) + half * HALF
        return pl.ds(pl.multiple_of(start, HALF), HALF)

    def copy(rows, send, recv, peer):
        return pltpu.make_async_remote_copy(
            src_ref=cond.at[rows], dst_ref=cond.at[rows], send_sem=send, recv_sem=recv,
            device_id=peer, device_id_type=MESH,
        )

    def stream_rows(stream, place):
        return rows_at(place, 1 - h if stream == 2 else h, c, 0 if stream == 0 else 1)

    def y_copy(stream, up, step):
        src_place = 0 if isinstance(step, int) and step == 0 else 2 * step - 1 + up
        index = (step * 3 + stream) * 2 + up
        return pltpu.make_async_remote_copy(
            src_ref=cond.at[stream_rows(stream, src_place)],
            dst_ref=cond.at[stream_rows(stream, 2 * (step + 1) - 1 + up)],
            send_sem=y_send.at[index], recv_sem=y_recv.at[index],
            device_id=y_prev if up else y_next, device_id_type=MESH,
        )

    def y4_copy(stream):
        down = lax.rem(c + stream, 2)
        peer = lax.rem(y + jnp.where(down == 1, NY - 1, 1), NY)
        return pltpu.make_async_remote_copy(
            src_ref=cond.at[stream_rows(stream, 5 + down)], dst_ref=cond.at[stream_rows(stream, 7)],
            send_sem=y4_send.at[stream], recv_sem=y4_recv.at[stream],
            device_id=device(peer, h, c, lo, z), device_id_type=MESH,
        )

    def x_copy(place, own, half=0):
        index = place if half == 0 else NY
        return copy(rows_at(place, h if own else 1 - h, c, half), x_send.at[index], x_recv.at[index], x_peer)

    def s_copy(place, hh_own, half, own):
        hh = h if hh_own else 1 - h
        index = (place * NH + (0 if hh_own else 1)) * 2 + half
        return copy(rows_at(place, hh, c if own else 1 - c, half), s_send.at[index], s_recv.at[index], sibling)

    mats = weights(bi_ref, bo_ref, eig_ref)
    loads[0].wait()
    for half in range(2):
        pieces = precondition(q_ref[half * HALF : (half + 1) * HALF, :], mats, rows_ref, turned_ref)
        for p, piece in enumerate(pieces):
            cond[rows_at(0, h, c, half), p * LANES : (p + 1) * LANES] = piece
        if half == 0:
            pl.semaphore_wait(barrier, 12)
        else:
            x_copy(0, True, 1).start()
        y_copy(half, 0, 0).start()
        y_copy(half, 1, 0).start()
        if half == 0:
            x_copy(0, True).start()
        s_copy(0, True, half, True).start()
    x_copy(0, False, 1).wait_recv()
    y_copy(2, 0, 0).start()
    y_copy(2, 1, 0).start()
    s_copy(0, False, 1, True).start()
    x_copy(0, False).wait_recv()
    s_copy(0, False, 0, True).start()

    def z_copy(place, hh, zm, blk):
        return pltpu.make_async_remote_copy(
            src_ref=outbox.at[pl.ds(pl.multiple_of((place * NH + hh) * BLOCK, BLOCK), BLOCK)],
            dst_ref=inbox.at[blk, z],
            send_sem=z_send.at[place * NH + hh], recv_sem=z_recv.at[blk * NZ + z],
            device_id=device(y, h, c, lo, zm), device_id_type=MESH,
        )

    def owner(place, hh):
        if isinstance(place, int) and place == 0:
            from_y = y
        elif isinstance(place, int):
            from_y = lax.rem(y + 4, NY)
        else:
            step, down = (place + 1) // 2, lax.rem(place + 1, 2)
            from_y = lax.rem(y + jnp.where(down == 1, step, NY - step), NY)
        m = from_y * NH + hh
        return lax.rem(m, NZ), m // NZ

    def multiply(place, places):
        count = places * NH * BLOCK
        rows = pl.ds(pl.multiple_of(place * NH * BLOCK, BLOCK), count)
        outbox[rows, :] = dot(cond[rows, :], t_ref[...], ((1,), (1,))).astype(BF16)
        for k in range(places):
            for hh in range(NH):
                zm, blk = owner(place + k, hh)

                @pl.when(zm != z)
                def _():
                    z_copy(place + k, hh, zm, blk).start()

                @pl.when(zm == z)
                def _():
                    rows = pl.ds(pl.multiple_of(((place + k) * NH + hh) * BLOCK, BLOCK), BLOCK)
                    inbox[blk, z] = outbox[rows, :]

    def wait_sibling(place):
        for own_h in (True, False):
            for half in range(2):
                s_copy(place, own_h, half, False).wait_recv()

    loads[1].wait()
    wait_sibling(0)
    multiply(0, 1)

    for step in range(1, 4):
        for stream in range(3):
            for up in range(2):
                y_copy(stream, up, step - 1).wait_recv()
                if step < 3:
                    y_copy(stream, up, step).start()
            if step == 3:
                y4_copy(stream).start()
            for up in range(2):
                place = 2 * step - 1 + up
                if stream == 0:
                    x_copy(place, True).start()
                s_copy(place, stream != 2, 0 if stream == 0 else 1, True).start()
        for up in range(2):
            place = 2 * step - 1 + up
            x_copy(place, False).wait_recv()
            s_copy(place, False, 0, True).start()
        for up in range(2):
            wait_sibling(2 * step - 1 + up)
        multiply_at = jnp.int32(2 * step - 1)
        multiply(multiply_at, 2)

    for stream in range(3):
        y4_copy(stream).wait_recv()
        if stream == 0:
            x_copy(7, True).start()
        s_copy(7, stream != 2, 0 if stream == 0 else 1, True).start()
    x_copy(7, False).wait_recv()
    s_copy(7, False, 0, True).start()
    wait_sibling(7)
    multiply(7, 1)

    def collect(blk):
        def await_one(k, _):
            frm = lax.rem(z + k, NZ)
            pltpu.make_async_remote_copy(
                src_ref=inbox.at[blk, frm], dst_ref=inbox.at[blk, frm],
                send_sem=z_send.at[0], recv_sem=z_recv.at[blk * NZ + frm],
                device_id=device(y, h, c, lo, frm), device_id_type=MESH,
            ).wait_recv()
            return 0

        lax.fori_loop(1, NZ, await_one, 0)
        total = inbox[blk, 0].astype(F32)
        for k in range(1, NZ):
            total += inbox[blk, k].astype(F32)
        return total

    l_copy = pltpu.make_async_remote_copy(
        src_ref=sums, dst_ref=xbox, send_sem=l_send, recv_sem=l_recv, device_id=lo_peer, device_id_type=MESH
    )
    sums[...] = collect(1 - lo)
    l_copy.start()
    mine = collect(lo)
    l_copy.wait_recv()
    out_ref[...] = mine + xbox[...]

    l_copy.wait_send()
    for stream in range(3):
        for step in range(3):
            for up in range(2):
                y_copy(stream, up, step).wait_send()
        y4_copy(stream).wait_send()
    for place in range(NY):
        x_copy(place, True).wait_send()
        for own_h in (True, False):
            for half in range(2):
                s_copy(place, own_h, half, True).wait_send()
    x_copy(0, True, 1).wait_send()
    for place in range(NY):
        for hh in range(NH):
            zm, blk = owner(place if place in (0, 7) else jnp.int32(place), hh)

            @pl.when(zm != z)
            def _():
                z_copy(place, hh, zm, blk).wait_send()


def per_device(queries, train_grads, basis_in, basis_out, inverse_eigen):
    any_space = pl.BlockSpec(memory_space=pl.ANY)
    vmem = pl.BlockSpec(memory_space=pltpu.VMEM)
    dma = pltpu.SemaphoreType.DMA
    return pl.pallas_call(
        kernel,
        out_shape=jax.ShapeDtypeStruct((BLOCK, COLS), F32),
        in_specs=[any_space, any_space, vmem, vmem, vmem],
        out_specs=vmem,
        scratch_shapes=[
            pltpu.VMEM((2 * HALF, GRAD), BF16),
            pltpu.VMEM((COLS, GRAD), BF16),
            pltpu.VMEM((NY * NH * BLOCK, GRAD), BF16),
            pltpu.VMEM((NY * NH * BLOCK, COLS), BF16),
            pltpu.VMEM((NL, NZ, BLOCK, COLS), BF16),
            pltpu.VMEM((BLOCK, COLS), F32),
            pltpu.VMEM((BLOCK, COLS), F32),
            pltpu.VMEM((PAIRS * HALF, LANES), F32),
            pltpu.VMEM((PAIRS * HALF, LANES), F32),
            dma((2,)),
            dma((18,)), dma((18,)),
            dma((3,)), dma((3,)),
            dma((9,)), dma((9,)),
            dma((32,)), dma((32,)),
            dma((16,)), dma((16,)),
            dma, dma,
        ],
        compiler_params=pltpu.CompilerParams(
            collective_id=0, has_side_effects=True, vmem_limit_bytes=40 * 1024 * 1024
        ),
        cost_estimate=pl.CostEstimate(
            flops=2 * 1024 * GRAD * COLS, bytes_accessed=5 * 1024 * 1024, transcendentals=0
        ),
        name="influence",
    )(queries, train_grads, basis_in[0], basis_out[0], inverse_eigen[0])


def solution(mesh):
    in_specs = (
        P("layer", "ex", None),
        P("layer", "ex", None),
        P("layer", None, None),
        P("layer", None, None),
        P("layer", None, None),
    )
    out_specs = P("layer", "ex")
    return jax.shard_map(
        per_device, mesh=mesh, in_specs=in_specs, out_specs=out_specs, check_vma=False
    )
```

time: 220 us -> 84 us (0.38)
  the two profiles are of different devices: /device:TPU:8 before, /device:TPU:66 now
where the time goes in v1:
time: 84 us; the launch traced here: 83.6 us
  Pallas kernels  77.6 us (92%)
  local copies, waits for them, and re-layouts  6.07 us (7%)
    pallas_call x1, Pallas kernels, per_device(): pl.pallas_call(kernel, out_shape=jax.ShapeDtypeStruct((BLOCK, COLS), F32)...  77.6 us
    unnamed x11, local copies, waits for them, and re-layouts  6.07 us

profile of v1, /device:TPU:66, one launch (start us, length us, event | category | flops | bytes accessed | tf_op | source)
XLA Modules:
  0.0 83.6 jit_solution(16640940973441811148)
XLA Ops:
  0.0 0.0 copy-start
  0.0 2.2 %copy-done = bf16[1,512,4096]{2,1,0:T(8,128)(2,1)S(1)} copy-done((bf16[1,512,4096]{2,1,0:T(8,128)(2,1)S(1)}, bf16[1,512,4096]{2,1,0:T(8,128)(2,1)}, u32[]{:S(2)}) %copy-start) | copy-done | bytes 4194328
  2.2 0.0 copy-start.1
  2.2 0.9 %copy-done.1 = bf16[1,32,4096]{2,1,0:T(8,128)(2,1)S(1)} copy-done((bf16[1,32,4096]{2,1,0:T(8,128)(2,1)S(1)}, bf16[1,32,4096]{2,1,0:T(8,128)(2,1)}, u32[]{:S(2)}) %copy-start.1) | copy-done | bytes 262168
  3.1 0.0 copy-start.2
  3.1 0.8 copy-done.2
  3.9 0.0 copy-start.3
  3.9 0.8 copy-done.3
  4.7 0.0 copy-start.4
  4.7 0.8 copy-done.4
  5.4 77.6 %influence.1 = f32[64,512]{1,0:T(8,128)S(1)} custom-call(bf16[1,32,4096]{2,1,0:T(8,128)(2,1)S(1)} %copy-done.1, bf16[1,512,4096]{2,1,0:T(8,128)(2,1)S(1)} %copy-done, f32[64,64]{1,0:T(8,128)S(1)} %bitcast.3, f32[64,64]{1,0:T(8,128)S(1)} %bitcast.4, f32[64,64]{1,0:T(8,128)S(1)} %bitcast.5), custom_call_target="tpu_custom_call" | custom-call | flops 4294967296 | bytes 5242880 | tf_op jit(solution)/shard_map/influence/pallas_call | solution.py:309
  83.0 0.7 copy.7
Async XLA Ops:
  0.0 2.2 %copy-start = (bf16[1,512,4096]{2,1,0:T(8,128)(2,1)S(1)}, bf16[1,512,4096]{2,1,0:T(8,128)(2,1)}, u32[]{:S(2)}) copy-start(bf16[1,512,4096]{2,1,0:T(8,128)(2,1)} %t_hbm.1) | copy-start | bytes 12582916
  2.2 0.9 %copy-start.1 = (bf16[1,32,4096]{2,1,0:T(8,128)(2,1)S(1)}, bf16[1,32,4096]{2,1,0:T(8,128)(2,1)}, u32[]{:S(2)}) copy-start(bf16[1,32,4096]{2,1,0:T(8,128)(2,1)} %q_hbm.1) | copy-start | bytes 786436
  3.1 0.8 copy-start.2
  3.9 0.8 copy-start.3
  4.7 0.8 copy-start.4

commit v2 on v1

v2 whole, which is shorter than its diff:
```python
import functools

import jax
import jax.numpy as jnp
from jax import lax
from jax.experimental import pallas as pl
from jax.experimental.pallas import tpu as pltpu
from jax.sharding import PartitionSpec as P

MESH = pl.DeviceIdType.MESH
NY, NH, NC = 8, 2, 2
NL, NZ = 2, 8
HALF = 16
WIDTH = 64
GRAD = WIDTH * WIDTH
LANES = 128
PAIRS = GRAD // LANES
BLOCK = 64
COLS = 512
F32, BF16 = jnp.float32, jnp.bfloat16


def split(value):
    high = value.astype(BF16)
    return high, (value - high.astype(F32)).astype(BF16)


def dot(left, right, dims=((1,), (0,))):
    return lax.dot_general(left, right, (dims, ((), ())), preferred_element_type=F32)


def twice(value):
    return jnp.concatenate([value, value], axis=1)


def lower_half(shape):
    return lax.rem(lax.broadcasted_iota(jnp.int32, shape, 1), LANES) < WIDTH


def weights(bi_ref, bo_ref, eig_ref):
    wide = twice(bi_ref[...])
    low = lower_half(wide.shape)
    diag = jnp.concatenate([jnp.where(low, wide, 0.0), jnp.where(low, 0.0, wide)], axis=0)
    diag_hi, diag_lo = split(diag)
    first = jnp.concatenate([diag_hi, diag_lo], axis=0)
    last = jnp.concatenate([diag_hi, diag_hi, diag_lo], axis=1)
    even, odd = bo_ref[pl.ds(0, PAIRS, stride=2), :], bo_ref[pl.ds(1, PAIRS, stride=2), :]
    rows = jnp.concatenate([even, odd], axis=1)
    rows_hi = rows.astype(BF16).astype(F32)
    rows_lo = rows - rows_hi
    into = jnp.transpose(jnp.concatenate([rows_hi, rows_hi, rows_lo, rows_lo], axis=0)).astype(BF16)
    stack = jnp.concatenate([even, odd], axis=0)
    stack_hi = stack.astype(BF16).astype(F32)
    back = jnp.concatenate([twice(stack_hi), twice(stack - stack_hi)], axis=1).astype(BF16)
    return first, into, twice(eig_ref[...]), back, last


def precondition(block, mats, rows_ref, turned_ref):
    first, into, eig, back, last = mats
    stacked = jnp.concatenate([block[:, p * LANES : (p + 1) * LANES] for p in range(PAIRS)], axis=0)
    rows_ref[...] = dot(jnp.concatenate([stacked, stacked], axis=1), first)
    right = jnp.concatenate([rows_ref[pl.ds(q, PAIRS, stride=HALF), :] for q in range(HALF)], axis=1)
    right_hi, right_lo = split(right)
    both = dot(into, jnp.concatenate([right_hi, right_lo, right_hi, right_lo], axis=0))
    low = lower_half((WIDTH, HALF * LANES))
    picked = jnp.where(low, both[:WIDTH], both[WIDTH:])
    scaled = []
    for q in range(HALF):
        part = picked[:, q * LANES : (q + 1) * LANES]
        scaled.append((part + pltpu.roll(part, WIDTH, 1)) * eig)
    scaled_hi, scaled_lo = split(jnp.concatenate(scaled, axis=1))
    left = dot(back, jnp.concatenate([scaled_hi, scaled_lo, scaled_hi, scaled_lo], axis=0))
    left = jnp.where(lower_half((PAIRS, HALF * LANES)), left[:PAIRS], left[PAIRS:])
    left = jnp.concatenate([left[:, q * LANES : (q + 1) * LANES] for q in range(HALF)], axis=0)
    left_hi, left_lo = split(left)
    full = dot(jnp.concatenate([left_hi, left_lo, left_hi], axis=1), last, ((1,), (1,)))
    for q in range(HALF):
        turned_ref[pl.ds(q, PAIRS, stride=HALF), :] = full[q * PAIRS : (q + 1) * PAIRS]
    return [turned_ref[p * HALF : (p + 1) * HALF, :].astype(BF16) for p in range(PAIRS)]


def kernel(
    q_hbm, t_hbm, bi_hbm, bo_hbm, eig_hbm, out_ref,
    q_ref, t_ref, bi_ref, bo_ref, eig_ref, cond, outbox, inbox, xbox, sums, rows_ref, turned_ref,
    load_sem, y_send, y_recv, y4_send, y4_recv, x_send, x_recv, s_send, s_recv, z_send, z_recv, l_send, l_recv,
):
    ex, layer = lax.axis_index("ex"), lax.axis_index("layer")
    y, h, c = ex // (NH * NC), lax.rem(ex // NC, NH), lax.rem(ex, NC)
    lo, z = layer // NZ, lax.rem(layer, NZ)

    def device(yy, hh, cc, ll, zz):
        return ((yy * NH + hh) * NC + cc, ll * NZ + zz)

    y_next = device(lax.rem(y + 1, NY), h, c, lo, z)
    y_prev = device(lax.rem(y + NY - 1, NY), h, c, lo, z)
    x_peer = device(y, 1 - h, c, lo, z)
    sibling = device(y, h, 1 - c, lo, z)
    lo_peer = device(y, h, c, 1 - lo, z)

    with jax.named_scope("greet"):
        barrier = pltpu.get_barrier_semaphore()
        for peer in (y_next, y_prev, x_peer, sibling, lo_peer):
            pl.semaphore_signal(barrier, inc=1, device_id=peer, device_id_type=MESH)

        def greet(k, _):
            pl.semaphore_signal(
                barrier, inc=1, device_id=device(y, h, c, lo, lax.rem(z + k, NZ)), device_id_type=MESH
            )
            return 0

        lax.fori_loop(1, NZ, greet, 0)
        pairs = [(q_hbm, q_ref), (bi_hbm, bi_ref), (bo_hbm, bo_ref), (eig_hbm, eig_ref), (t_hbm, t_ref)]
        loads = [pltpu.make_async_copy(src.at[0], dst, load_sem.at[i]) for i, (src, dst) in enumerate(pairs)]
        for load in loads:
            load.start()

    def place_rows(half, place, count):
        start = (half * NY + place) * (NH * NC * HALF)
        return pl.ds(start, count * NH * NC * HALF)

    def rows_at(place, hh, cc, half):
        start = (((half * NY + place) * NH + hh) * NC + cc) * HALF
        return pl.ds(pl.multiple_of(start, HALF), HALF)

    def copy(rows, send, recv, peer):
        return pltpu.make_async_remote_copy(
            src_ref=cond.at[rows], dst_ref=cond.at[rows], send_sem=send, recv_sem=recv,
            device_id=peer, device_id_type=MESH,
        )

    def stream_rows(stream, place):
        return rows_at(place, 1 - h if stream == 2 else h, c, 0 if stream == 0 else 1)

    def y_copy(stream, up, step):
        src_place = 0 if step == 0 else 2 * step - 1 + up
        index = (step * 3 + stream) * 2 + up
        return pltpu.make_async_remote_copy(
            src_ref=cond.at[stream_rows(stream, src_place)],
            dst_ref=cond.at[stream_rows(stream, 2 * (step + 1) - 1 + up)],
            send_sem=y_send.at[index], recv_sem=y_recv.at[index],
            device_id=y_prev if up else y_next, device_id_type=MESH,
        )

    def y4_copy(stream):
        down = lax.rem(c + stream, 2)
        peer = lax.rem(y + jnp.where(down == 1, NY - 1, 1), NY)
        return pltpu.make_async_remote_copy(
            src_ref=cond.at[stream_rows(stream, 5 + down)], dst_ref=cond.at[stream_rows(stream, 7)],
            send_sem=y4_send.at[stream], recv_sem=y4_recv.at[stream],
            device_id=device(peer, h, c, lo, z), device_id_type=MESH,
        )

    def x_copy(place, own, half=0):
        index = place if half == 0 else NY
        return copy(rows_at(place, h if own else 1 - h, c, half), x_send.at[index], x_recv.at[index], x_peer)

    def s_copy(place, hh_own, half, own):
        hh = h if hh_own else 1 - h
        index = (place * NH + (0 if hh_own else 1)) * 2 + half
        return copy(rows_at(place, hh, c if own else 1 - c, half), s_send.at[index], s_recv.at[index], sibling)

    def z_copy(half, place, hh, zm, blk):
        index = (half * NY + place) * NH + hh
        rows = pl.ds(pl.multiple_of(index * (NC * HALF), NC * HALF), NC * HALF)
        return pltpu.make_async_remote_copy(
            src_ref=outbox.at[rows], dst_ref=inbox.at[blk, half, z],
            send_sem=z_send.at[index], recv_sem=z_recv.at[(blk * 2 + half) * NZ + z],
            device_id=device(y, h, c, lo, zm), device_id_type=MESH,
        )

    def owner(place, hh):
        shift = (0, 7, 1, 6, 2, 5, 3, 4)[place]
        m = lax.rem(y + shift, NY) * NH + hh
        return lax.rem(m, NZ), m // NZ

    def wait_sibling(half, place):
        for hh_own in (True, False):
            s_copy(place, hh_own, half, False).wait_recv()

    def multiply(half, place, places):
        with jax.named_scope(f"await_{half}_{place}"):
            for k in range(places):
                wait_sibling(half, place + k)
        with jax.named_scope(f"multiply_{half}_{place}"):
            rows = place_rows(half, place, places)
            outbox[rows, :] = dot(cond[rows, :], t_ref[...], ((1,), (1,))).astype(BF16)
            for k in range(places):
                for hh in range(NH):
                    zm, blk = owner(place + k, hh)

                    @pl.when(zm != z)
                    def _():
                        z_copy(half, place + k, hh, zm, blk).start()

                    @pl.when(zm == z)
                    def _():
                        start = ((half * NY + place + k) * NH + hh) * (NC * HALF)
                        inbox[blk, half, z] = outbox[start : start + NC * HALF, :]

    def arrive(stream, step):
        with jax.named_scope(f"y_{stream}_{step}"):
            for up in range(2):
                y_copy(stream, up, step - 1).wait_recv()
                if step < 3:
                    y_copy(stream, up, step).start()
            if step == 3:
                y4_copy(stream).start()
            for up in range(2):
                place = 2 * step - 1 + up
                if stream == 0:
                    x_copy(place, True).start()
                s_copy(place, stream != 2, 0 if stream == 0 else 1, True).start()

    def arrive_far(stream):
        with jax.named_scope(f"y_{stream}_4"):
            y4_copy(stream).wait_recv()
            if stream == 0:
                x_copy(7, True).start()
            s_copy(7, stream != 2, 0 if stream == 0 else 1, True).start()

    def arrive_x(*places):
        with jax.named_scope(f"x_{places[0]}"):
            for place in places:
                x_copy(place, False).wait_recv()
                s_copy(place, False, 0, True).start()

    def condition(half):
        pieces = precondition(q_ref[half * HALF : (half + 1) * HALF, :], mats, rows_ref, turned_ref)
        for p, piece in enumerate(pieces):
            cond[rows_at(0, h, c, half), p * LANES : (p + 1) * LANES] = piece

    with jax.named_scope("load"):
        for load in loads[:4]:
            load.wait()
    with jax.named_scope("condition_0"):
        mats = weights(bi_ref, bo_ref, eig_ref)
        condition(0)
    with jax.named_scope("barrier"):
        pl.semaphore_wait(barrier, 12)
    y_copy(0, 0, 0).start()
    y_copy(0, 1, 0).start()
    with jax.named_scope("condition_1"):
        condition(1)
    x_copy(0, True, 1).start()
    y_copy(1, 0, 0).start()
    y_copy(1, 1, 0).start()
    x_copy(0, True).start()
    s_copy(0, True, 0, True).start()
    s_copy(0, True, 1, True).start()
    with jax.named_scope("x_other"):
        x_copy(0, False, 1).wait_recv()
    y_copy(2, 0, 0).start()
    y_copy(2, 1, 0).start()
    s_copy(0, False, 1, True).start()
    arrive_x(0)
    with jax.named_scope("load_train"):
        loads[4].wait()

    for step in range(1, 4):
        place, places = (2 * step - 3, 2) if step > 1 else (0, 1)
        arrive(0, step)
        multiply(0, place, places)
        arrive(1, step)
        multiply(1, place, places)
        arrive(2, step)
        arrive_x(2 * step - 1, 2 * step)
    arrive_far(0)
    multiply(0, 5, 2)
    arrive_far(1)
    arrive_far(2)
    multiply(1, 5, 2)
    arrive_x(7)
    multiply(0, 7, 1)
    multiply(1, 7, 1)

    with jax.named_scope("drain"):
        for stream in range(3):
            for step in range(3):
                for up in range(2):
                    y_copy(stream, up, step).wait_send()
            y4_copy(stream).wait_send()
        for place in range(NY):
            x_copy(place, True).wait_send()
            for hh_own in (True, False):
                for half in range(2):
                    s_copy(place, hh_own, half, True).wait_send()
        x_copy(0, True, 1).wait_send()

    def collect(blk, half):
        def await_one(k, _):
            frm = lax.rem(z + k, NZ)
            pltpu.make_async_remote_copy(
                src_ref=inbox.at[blk, half, frm], dst_ref=inbox.at[blk, half, frm],
                send_sem=z_send.at[0], recv_sem=z_recv.at[(blk * 2 + half) * NZ + frm],
                device_id=device(y, h, c, lo, frm), device_id_type=MESH,
            ).wait_recv()
            return 0

        lax.fori_loop(1, NZ, await_one, 0)
        total = inbox[blk, half, 0].astype(F32)
        for k in range(1, NZ):
            total += inbox[blk, half, k].astype(F32)
        return total

    def l_copy(half):
        return pltpu.make_async_remote_copy(
            src_ref=sums.at[half], dst_ref=xbox.at[half], send_sem=l_send.at[half], recv_sem=l_recv.at[half],
            device_id=lo_peer, device_id_type=MESH,
        )

    with jax.named_scope("collect_other"):
        for half in range(2):
            sums[half] = collect(1 - lo, half)
            l_copy(half).start()
    with jax.named_scope("collect_own"):
        mine = [collect(lo, half) for half in range(2)]
    with jax.named_scope("finish"):
        for half in range(2):
            l_copy(half).wait_recv()
            total = mine[half] + xbox[half]
            for cc in range(NC):
                out_ref[(cc * 2 + half) * HALF : (cc * 2 + half + 1) * HALF, :] = total[cc * HALF : (cc + 1) * HALF]
    with jax.named_scope("drain_sums"):
        for half in range(2):
            l_copy(half).wait_send()
            for place in range(NY):
                for hh in range(NH):
                    zm, blk = owner(place, hh)

                    @pl.when(zm != z)
                    def _():
                        z_copy(half, place, hh, zm, blk).wait_send()


def per_device(queries, train_grads, basis_in, basis_out, inverse_eigen):
    any_space = pl.BlockSpec(memory_space=pl.ANY)
    vmem = pl.BlockSpec(memory_space=pltpu.VMEM)
    dma = pltpu.SemaphoreType.DMA
    return pl.pallas_call(
        kernel,
        out_shape=jax.ShapeDtypeStruct((BLOCK, COLS), F32),
        in_specs=[any_space] * 5,
        out_specs=vmem,
        scratch_shapes=[
            pltpu.VMEM((2 * HALF, GRAD), BF16),
            pltpu.VMEM((COLS, GRAD), BF16),
            pltpu.VMEM((WIDTH, WIDTH), F32),
            pltpu.VMEM((WIDTH, WIDTH), F32),
            pltpu.VMEM((WIDTH, WIDTH), F32),
            pltpu.VMEM((NY * NH * BLOCK, GRAD), BF16),
            pltpu.VMEM((NY * NH * BLOCK, COLS), BF16),
            pltpu.VMEM((NL, 2, NZ, NC * HALF, COLS), BF16),
            pltpu.VMEM((2, NC * HALF, COLS), F32),
            pltpu.VMEM((2, NC * HALF, COLS), F32),
            pltpu.VMEM((PAIRS * HALF, LANES), F32),
            pltpu.VMEM((PAIRS * HALF, LANES), F32),
            dma((5,)),
            dma((18,)), dma((18,)),
            dma((3,)), dma((3,)),
            dma((9,)), dma((9,)),
            dma((32,)), dma((32,)),
            dma((32,)), dma((32,)),
            dma((2,)), dma((2,)),
        ],
        compiler_params=pltpu.CompilerParams(
            collective_id=0, has_side_effects=True, vmem_limit_bytes=60 * 1024 * 1024
        ),
        cost_estimate=pl.CostEstimate(
            flops=2 * 1024 * GRAD * COLS, bytes_accessed=5 * 1024 * 1024, transcendentals=0
        ),
        name="influence",
    )(queries, train_grads, basis_in, basis_out, inverse_eigen)


def solution(mesh):
    in_specs = (
        P("layer", "ex", None),
        P("layer", "ex", None),
        P("layer", None, None),
        P("layer", None, None),
        P("layer", None, None),
    )
    out_specs = P("layer", "ex")
    return jax.shard_map(
        per_device, mesh=mesh, in_specs=in_specs, out_specs=out_specs, check_vma=False
    )
```

time: 84 us -> 69.5 us (0.83)
  the two profiles are of different devices: /device:TPU:66 before, /device:TPU:2 now
where the time goes in v2:
time: 69.5 us; the launch traced here: 69.1 us
  Pallas kernels  67.5 us (97%)
  local copies, waits for them, and re-layouts  1.57 us (2%)
    pallas_call x1, Pallas kernels, per_device(): pl.pallas_call(kernel, out_shape=jax.ShapeDtypeStruct((BLOCK, COLS), F32)...  67.5 us
    unnamed x1, local copies, waits for them, and re-layouts  1.57 us

profile of v2, /device:TPU:2, one launch (start us, length us, event | category | flops | bytes accessed | tf_op | source)
XLA Modules:
  0.0 69.1 jit_solution(16791470884837533841)
XLA Ops:
  0.0 67.5 %influence.1 = f32[64,512]{1,0:T(8,128)} custom-call(bf16[1,32,4096]{2,1,0:T(8,128)(2,1)} %q_hbm.1, bf16[1,512,4096]{2,1,0:T(8,128)(2,1)} %t_hbm.1, f32[1,64,64]{2,1,0:T(8,128)} %bi_hbm.1, f32[1,64,64]{2,1,0:T(8,128)} %bo_hbm.1, f32[1,64,64]{2,1,0:T(8,128)} %eig_hbm.1), custom_call_target="tpu_custom_call" | custom-call | flops 4294967296 | bytes 5242880 | tf_op jit(solution)/shard_map/influence/pallas_call | solution.py:339
  67.5 1.6 %copy.7 = f32[64,512]{1,0:T(8,128)} copy(f32[64,512]{1,0:T(8,128)} %influence.1) | data formatting | bytes 262144

commit v3 on v2

--- a/solution.py
+++ b/solution.py
@@ -98,21 +98,18 @@
     lo_peer = device(y, h, c, 1 - lo, z)
 
     with jax.named_scope("greet"):
+        pairs = [(q_hbm, q_ref), (bi_hbm, bi_ref), (bo_hbm, bo_ref), (eig_hbm, eig_ref), (t_hbm, t_ref)]
+        loads = [pltpu.make_async_copy(src.at[0], dst, load_sem.at[i]) for i, (src, dst) in enumerate(pairs)]
+        for load in loads[:4]:
+            load.start()
         barrier = pltpu.get_barrier_semaphore()
         for peer in (y_next, y_prev, x_peer, sibling, lo_peer):
             pl.semaphore_signal(barrier, inc=1, device_id=peer, device_id_type=MESH)
-
-        def greet(k, _):
+        loads[4].start()
+        for k in range(1, NZ):
             pl.semaphore_signal(
                 barrier, inc=1, device_id=device(y, h, c, lo, lax.rem(z + k, NZ)), device_id_type=MESH
             )
-            return 0
-
-        lax.fori_loop(1, NZ, greet, 0)
-        pairs = [(q_hbm, q_ref), (bi_hbm, bi_ref), (bo_hbm, bo_ref), (eig_hbm, eig_ref), (t_hbm, t_ref)]
-        loads = [pltpu.make_async_copy(src.at[0], dst, load_sem.at[i]) for i, (src, dst) in enumerate(pairs)]
-        for load in loads:
-            load.start()
 
     def place_rows(half, place, count):
         start = (half * NY + place) * (NH * NC * HALF)
@@ -173,17 +170,43 @@
         m = lax.rem(y + shift, NY) * NH + hh
         return lax.rem(m, NZ), m // NZ
 
-    def wait_sibling(half, place):
-        for hh_own in (True, False):
-            s_copy(place, hh_own, half, False).wait_recv()
-
-    def multiply(half, place, places):
+    def multiply(half, place, places, hh_own=None):
         with jax.named_scope(f"await_{half}_{place}"):
             for k in range(places):
-                wait_sibling(half, place + k)
+                for own in (True, False) if hh_own is None else (hh_own,):
+                    s_copy(place + k, own, half, False).wait_recv()
         with jax.named_scope(f"multiply_{half}_{place}"):
-            rows = place_rows(half, place, places)
+            if hh_own is None:
+                rows, parts = place_rows(half, place, places), range(NH)
+            else:
+                parts = (h if hh_own else 1 - h,)
+                start = ((half * NY + place) * NH + parts[0]) * (NC * HALF)
+                rows = pl.ds(pl.multiple_of(start, NC * HALF), NC * HALF)
             outbox[rows, :] = dot(cond[rows, :], t_ref[...], ((1,), (1,))).astype(BF16)
+            for k in range(places):
+                for hh in parts:
+                    zm, blk = owner(place + k, hh)
+
+                    @pl.when(zm != z)
+                    def _():
+                        z_copy(half, place + k, hh, zm, blk).start()
+
+                    @pl.when(zm == z)
+                    def _():
+                        start = pl.multiple_of(((half * NY + place + k) * NH + hh) * (NC * HALF), NC * HALF)
+                        inbox[blk, half, z] = outbox[pl.ds(start, NC * HALF), :]
+
+    def multiply_both(place, places):
+        for half in range(2):
+            for k in range(places):
+                for own in (True, False):
+                    s_copy(place + k, own, half, False).wait_recv()
+        count = places * NH * NC * HALF
+        rows = [place_rows(half, place, places) for half in range(2)]
+        product = dot(jnp.concatenate([cond[r, :] for r in rows], axis=0), t_ref[...], ((1,), (1,))).astype(BF16)
+        for half in range(2):
+            outbox[rows[half], :] = product[half * count : (half + 1) * count]
+        for half in range(2):
             for k in range(places):
                 for hh in range(NH):
                     zm, blk = owner(place + k, hh)
@@ -194,8 +217,8 @@
 
                     @pl.when(zm == z)
                     def _():
-                        start = ((half * NY + place + k) * NH + hh) * (NC * HALF)
-                        inbox[blk, half, z] = outbox[start : start + NC * HALF, :]
+                        start = pl.multiple_of(((half * NY + place + k) * NH + hh) * (NC * HALF), NC * HALF)
+                        inbox[blk, half, z] = outbox[pl.ds(start, NC * HALF), :]
 
     def arrive(stream, step):
         with jax.named_scope(f"y_{stream}_{step}"):
@@ -247,6 +270,7 @@
     x_copy(0, True).start()
     s_copy(0, True, 0, True).start()
     s_copy(0, True, 1, True).start()
+    arrive(0, 1)
     with jax.named_scope("x_other"):
         x_copy(0, False, 1).wait_recv()
     y_copy(2, 0, 0).start()
@@ -255,22 +279,28 @@
     arrive_x(0)
     with jax.named_scope("load_train"):
         loads[4].wait()
-
-    for step in range(1, 4):
-        place, places = (2 * step - 3, 2) if step > 1 else (0, 1)
-        arrive(0, step)
-        multiply(0, place, places)
-        arrive(1, step)
-        multiply(1, place, places)
-        arrive(2, step)
-        arrive_x(2 * step - 1, 2 * step)
+    multiply_both(0, 1)
+    arrive(0, 2)
+    arrive(1, 1)
+    arrive(2, 1)
+    arrive_x(1, 2)
+    multiply_both(1, 2)
+    arrive(0, 3)
+    arrive(1, 2)
+    arrive_x(3, 4)
+    multiply(0, 3, 2)
     arrive_far(0)
+    arrive(2, 2)
+    multiply(1, 3, 2)
+    arrive_x(5, 6)
+    arrive(1, 3)
     multiply(0, 5, 2)
+    arrive(2, 3)
+    arrive_x(7)
+    multiply(0, 7, 1)
+    multiply(1, 5, 2)
     arrive_far(1)
     arrive_far(2)
-    multiply(1, 5, 2)
-    arrive_x(7)
-    multiply(0, 7, 1)
     multiply(1, 7, 1)
 
     with jax.named_scope("drain"):
@@ -308,12 +338,13 @@
             device_id=lo_peer, device_id_type=MESH,
         )
 
-    with jax.named_scope("collect_other"):
-        for half in range(2):
+    mine = []
+    for half in range(2):
+        with jax.named_scope("collect_other"):
             sums[half] = collect(1 - lo, half)
             l_copy(half).start()
-    with jax.named_scope("collect_own"):
-        mine = [collect(lo, half) for half in range(2)]
+        with jax.named_scope("collect_own"):
+            mine.append(collect(lo, half))
     with jax.named_scope("finish"):
         for half in range(2):
             l_copy(half).wait_recv()
@@ -333,13 +364,13 @@
 
 
 def per_device(queries, train_grads, basis_in, basis_out, inverse_eigen):
-    any_space = pl.BlockSpec(memory_space=pl.ANY)
+    hbm = pl.BlockSpec(memory_space=pl.ANY)
     vmem = pl.BlockSpec(memory_space=pltpu.VMEM)
     dma = pltpu.SemaphoreType.DMA
     return pl.pallas_call(
         kernel,
         out_shape=jax.ShapeDtypeStruct((BLOCK, COLS), F32),
-        in_specs=[any_space] * 5,
+        in_specs=[hbm] * 5,
         out_specs=vmem,
         scratch_shapes=[
             pltpu.VMEM((2 * HALF, GRAD), BF16),

time: 69.5 us -> 66.5 us (0.957)
  Pallas kernels: 67.5 us -> 64.8 us
    pallas_call x1, Pallas kernels: 67.5 us -> 64.8 us  [per_device(): pl.pallas_call(kernel, out_shape=jax.ShapeDtypeStruct((BLOCK, COLS), F32)...]
where the time goes in v3:
time: 66.5 us; the launch traced here: 66.4 us
  Pallas kernels  64.8 us (97%)
  local copies, waits for them, and re-layouts  1.57 us (2%)
    pallas_call x1, Pallas kernels, per_device(): pl.pallas_call(kernel, out_shape=jax.ShapeDtypeStruct((BLOCK, COLS), F32)...  64.8 us
    unnamed x1, local copies, waits for them, and re-layouts  1.57 us

profile of v3, /device:TPU:2, one launch (start us, length us, event | category | flops | bytes accessed | tf_op | source)
XLA Modules:
  0.0 66.4 jit_solution(14983242315992100412)
XLA Ops:
  0.0 64.8 %influence.1 = f32[64,512]{1,0:T(8,128)} custom-call(bf16[1,32,4096]{2,1,0:T(8,128)(2,1)} %q_hbm.1, bf16[1,512,4096]{2,1,0:T(8,128)(2,1)} %t_hbm.1, f32[1,64,64]{2,1,0:T(8,128)} %bi_hbm.1, f32[1,64,64]{2,1,0:T(8,128)} %bo_hbm.1, f32[1,64,64]{2,1,0:T(8,128)} %eig_hbm.1), custom_call_target="tpu_custom_call" | custom-call | flops 4294967296 | bytes 5242880 | tf_op jit(solution)/shard_map/influence/pallas_call | solution.py:370
  64.8 1.6 %copy.7 = f32[64,512]{1,0:T(8,128)} copy(f32[64,512]{1,0:T(8,128)} %influence.1) | data formatting | bytes 262144

commit v4 on v3

--- a/solution.py
+++ b/solution.py
@@ -17,6 +17,8 @@
 PAIRS = GRAD // LANES
 BLOCK = 64
 COLS = 512
+TURN = 256
+SHIFTS = (0, 7, 1, 6, 2, 5, 3, 4)
 F32, BF16 = jnp.float32, jnp.bfloat16
 
 
@@ -81,7 +83,7 @@
 
 def kernel(
     q_hbm, t_hbm, bi_hbm, bo_hbm, eig_hbm, out_ref,
-    q_ref, t_ref, bi_ref, bo_ref, eig_ref, cond, outbox, inbox, xbox, sums, rows_ref, turned_ref,
+    q_ref, t_ref, turned_t, bi_ref, bo_ref, eig_ref, cond, outbox, inbox, xbox, sums, rows_ref, turned_ref,
     load_sem, y_send, y_recv, y4_send, y4_recv, x_send, x_recv, s_send, s_recv, z_send, z_recv, l_send, l_recv,
 ):
     ex, layer = lax.axis_index("ex"), lax.axis_index("layer")
@@ -165,36 +167,32 @@
             device_id=device(y, h, c, lo, zm), device_id_type=MESH,
         )
 
-    def owner(place, hh):
-        shift = (0, 7, 1, 6, 2, 5, 3, 4)[place]
+    def owner(shift, hh):
         m = lax.rem(y + shift, NY) * NH + hh
         return lax.rem(m, NZ), m // NZ
 
-    def multiply(half, place, places, hh_own=None):
-        with jax.named_scope(f"await_{half}_{place}"):
-            for k in range(places):
-                for own in (True, False) if hh_own is None else (hh_own,):
-                    s_copy(place + k, own, half, False).wait_recv()
-        with jax.named_scope(f"multiply_{half}_{place}"):
-            if hh_own is None:
-                rows, parts = place_rows(half, place, places), range(NH)
-            else:
-                parts = (h if hh_own else 1 - h,)
-                start = ((half * NY + place) * NH + parts[0]) * (NC * HALF)
-                rows = pl.ds(pl.multiple_of(start, NC * HALF), NC * HALF)
-            outbox[rows, :] = dot(cond[rows, :], t_ref[...], ((1,), (1,))).astype(BF16)
-            for k in range(places):
-                for hh in parts:
-                    zm, blk = owner(place + k, hh)
-
-                    @pl.when(zm != z)
-                    def _():
-                        z_copy(half, place + k, hh, zm, blk).start()
-
-                    @pl.when(zm == z)
-                    def _():
-                        start = pl.multiple_of(((half * NY + place + k) * NH + hh) * (NC * HALF), NC * HALF)
-                        inbox[blk, half, z] = outbox[pl.ds(start, NC * HALF), :]
+    def send_sums(half, place, places):
+        for k in range(places):
+            at, shift = place + k, SHIFTS[place + k]
+            for hh in range(NH):
+                zm, blk = owner(shift, hh)
+
+                @pl.when(zm != z)
+                def _():
+                    z_copy(half, at, hh, zm, blk).start()
+
+                @pl.when(zm == z)
+                def _():
+                    start = pl.multiple_of(((half * NY + at) * NH + hh) * (NC * HALF), NC * HALF)
+                    inbox[blk, half, z] = outbox[pl.ds(start, NC * HALF), :]
+
+    def multiply(half, place, places):
+        for k in range(places):
+            for own in (True, False):
+                s_copy(place + k, own, half, False).wait_recv()
+        rows = place_rows(half, place, places)
+        outbox[rows, :] = dot(cond[rows, :], turned_t[...]).astype(BF16)
+        send_sums(half, place, places)
 
     def multiply_both(place, places):
         for half in range(2):
@@ -203,22 +201,11 @@
                     s_copy(place + k, own, half, False).wait_recv()
         count = places * NH * NC * HALF
         rows = [place_rows(half, place, places) for half in range(2)]
-        product = dot(jnp.concatenate([cond[r, :] for r in rows], axis=0), t_ref[...], ((1,), (1,))).astype(BF16)
+        product = dot(jnp.concatenate([cond[r, :] for r in rows], axis=0), turned_t[...]).astype(BF16)
         for half in range(2):
             outbox[rows[half], :] = product[half * count : (half + 1) * count]
         for half in range(2):
-            for k in range(places):
-                for hh in range(NH):
-                    zm, blk = owner(place + k, hh)
-
-                    @pl.when(zm != z)
-                    def _():
-                        z_copy(half, place + k, hh, zm, blk).start()
-
-                    @pl.when(zm == z)
-                    def _():
-                        start = pl.multiple_of(((half * NY + place + k) * NH + hh) * (NC * HALF), NC * HALF)
-                        inbox[blk, half, z] = outbox[pl.ds(start, NC * HALF), :]
+            send_sums(half, place, places)
 
     def arrive(stream, step):
         with jax.named_scope(f"y_{stream}_{step}"):
@@ -275,10 +262,17 @@
         x_copy(0, False, 1).wait_recv()
     y_copy(2, 0, 0).start()
     y_copy(2, 1, 0).start()
+    with jax.named_scope("turn_train"):
+        loads[4].wait()
+
+        def turn_train(k, _):
+            part = pl.ds(pl.multiple_of(k * TURN, TURN), TURN)
+            turned_t[part, :] = t_ref[:, part].T
+            return 0
+
+        lax.fori_loop(0, GRAD // TURN, turn_train, 0)
     s_copy(0, False, 1, True).start()
     arrive_x(0)
-    with jax.named_scope("load_train"):
-        loads[4].wait()
     multiply_both(0, 1)
     arrive(0, 2)
     arrive(1, 1)
@@ -338,11 +332,22 @@
             device_id=lo_peer, device_id_type=MESH,
         )
 
+    def drain_sums(half):
+        for place in range(NY):
+            for hh in range(NH):
+                zm, blk = owner(SHIFTS[place], hh)
+
+                @pl.when(zm != z)
+                def _():
+                    z_copy(half, place, hh, zm, blk).wait_send()
+
     mine = []
     for half in range(2):
         with jax.named_scope("collect_other"):
             sums[half] = collect(1 - lo, half)
             l_copy(half).start()
+        with jax.named_scope("drain_z"):
+            drain_sums(half)
         with jax.named_scope("collect_own"):
             mine.append(collect(lo, half))
     with jax.named_scope("finish"):
@@ -354,13 +359,6 @@
     with jax.named_scope("drain_sums"):
         for half in range(2):
             l_copy(half).wait_send()
-            for place in range(NY):
-                for hh in range(NH):
-                    zm, blk = owner(place, hh)
-
-                    @pl.when(zm != z)
-                    def _():
-                        z_copy(half, place, hh, zm, blk).wait_send()
 
 
 def per_device(queries, train_grads, basis_in, basis_out, inverse_eigen):
@@ -375,6 +373,7 @@
         scratch_shapes=[
             pltpu.VMEM((2 * HALF, GRAD), BF16),
             pltpu.VMEM((COLS, GRAD), BF16),
+            pltpu.VMEM((GRAD, COLS), BF16),
             pltpu.VMEM((WIDTH, WIDTH), F32),
             pltpu.VMEM((WIDTH, WIDTH), F32),
             pltpu.VMEM((WIDTH, WIDTH), F32),

time: 66.5 us -> 64.3 us (0.967)
  Pallas kernels: 64.8 us -> 62.6 us
    pallas_call x1, Pallas kernels: 64.8 us -> 62.6 us  [per_device(): pl.pallas_call(kernel, out_shape=jax.ShapeDtypeStruct((BLOCK, COLS), F32)...]
where the time goes in v4:
time: 64.3 us; the launch traced here: 64.2 us
  Pallas kernels  62.6 us (97%)
  local copies, waits for them, and re-layouts  1.57 us (2%)
    pallas_call x1, Pallas kernels, per_device(): pl.pallas_call(kernel, out_shape=jax.ShapeDtypeStruct((BLOCK, COLS), F32)...  62.6 us
    unnamed x1, local copies, waits for them, and re-layouts  1.57 us

profile of v4, /device:TPU:2, one launch (start us, length us, event | category | flops | bytes accessed | tf_op | source)
XLA Modules:
  0.0 64.2 jit_solution(8700312145277304038)
XLA Ops:
  0.0 62.6 %influence.1 = f32[64,512]{1,0:T(8,128)} custom-call(bf16[1,32,4096]{2,1,0:T(8,128)(2,1)} %q_hbm.1, bf16[1,512,4096]{2,1,0:T(8,128)(2,1)} %t_hbm.1, f32[1,64,64]{2,1,0:T(8,128)} %bi_hbm.1, f32[1,64,64]{2,1,0:T(8,128)} %bo_hbm.1, f32[1,64,64]{2,1,0:T(8,128)} %eig_hbm.1), custom_call_target="tpu_custom_call" | custom-call | flops 4294967296 | bytes 5242880 | tf_op jit(solution)/shard_map/influence/pallas_call | solution.py:368
  62.6 1.6 %copy.7 = f32[64,512]{1,0:T(8,128)} copy(f32[64,512]{1,0:T(8,128)} %influence.1) | data formatting | bytes 262144

commit v5 on v4

--- a/solution.py
+++ b/solution.py
@@ -273,9 +273,9 @@
         lax.fori_loop(0, GRAD // TURN, turn_train, 0)
     s_copy(0, False, 1, True).start()
     arrive_x(0)
-    multiply_both(0, 1)
     arrive(0, 2)
     arrive(1, 1)
+    multiply_both(0, 1)
     arrive(2, 1)
     arrive_x(1, 2)
     multiply_both(1, 2)

time: 64.3 us -> 64.1 us (level)
  no operation moved by 1% of the time
where the time goes in v5:
time: 64.1 us; the launch traced here: 63.9 us
  Pallas kernels  62.4 us (97%)
  local copies, waits for them, and re-layouts  1.57 us (2%)
    pallas_call x1, Pallas kernels, per_device(): pl.pallas_call(kernel, out_shape=jax.ShapeDtypeStruct((BLOCK, COLS), F32)...  62.4 us
    unnamed x1, local copies, waits for them, and re-layouts  1.57 us

profile of v5, /device:TPU:2, one launch (start us, length us, event | category | flops | bytes accessed | tf_op | source)
XLA Modules:
  0.0 63.9 jit_solution(11487613971472593998)
XLA Ops:
  0.0 62.4 %influence.1 = f32[64,512]{1,0:T(8,128)} custom-call(bf16[1,32,4096]{2,1,0:T(8,128)(2,1)} %q_hbm.1, bf16[1,512,4096]{2,1,0:T(8,128)(2,1)} %t_hbm.1, f32[1,64,64]{2,1,0:T(8,128)} %bi_hbm.1, f32[1,64,64]{2,1,0:T(8,128)} %bo_hbm.1, f32[1,64,64]{2,1,0:T(8,128)} %eig_hbm.1), custom_call_target="tpu_custom_call" | custom-call | flops 4294967296 | bytes 5242880 | tf_op jit(solution)/shard_map/influence/pallas_call | solution.py:368
  62.4 1.6 %copy.7 = f32[64,512]{1,0:T(8,128)} copy(f32[64,512]{1,0:T(8,128)} %influence.1) | data formatting | bytes 262144
